TPU v7x, 256 devices: a whole 4x4x8 slice. The times are simulated.
256 devices in a mesh: sec: 8 (over x, y_lo), ctx: 32 (over z, y_hi, core).
Axes of the slice: x: 4, y: 4 (y_hi: 2, y_lo: 2; y = y_hi * 2 + y_lo), z: 8, core: 2. Of those that a mesh axis runs over, the one named last changes fastest.
Arguments:
- hidden_state: bfloat16 [8, 4096, 4096], P('sec', 'ctx'), may hold values from -8 to 8
- queries: bfloat16 [8, 4096, 4096], P('sec', 'ctx'), may hold values from -6 to 6
- key_vectors: bfloat16 [8, 4096, 4096], P('sec', 'ctx'), may hold values from -4.5 to 4.5
- value_vectors: bfloat16 [8, 4096, 4096], P('sec', 'ctx'), may hold values from -6 to 6
- modulation: float32 [32, 3, 4096], replicated, may hold values from -3 to 3
- down_weight: bfloat16 [4096, 256], replicated, may hold values from -0.09375 to 0.09375
- conv_weight: bfloat16 [3, 3, 3, 256, 256], replicated, may hold values from -0.078125 to 0.078125
- clip_frames: int32 [8], replicated, may hold values from 16 to 64, as said below
- destination: int32 [8], replicated, may hold values from 0 to 7, as said below
- timestep: int32 [8], replicated, may hold values from 0 to 31
Outputs:
- upsampled: bfloat16 [8, 4096, 256], P('sec', 'ctx')
Inputs may be any that keep to these rules, and one draw needn't show every extreme that they name: `clip_frames`: one section's clip fills all 64 frames. `destination`: every upsampler group receives exactly one clip; some group d receives the clip of section (d + 4) mod 8.
All inputs are finite; a program needn't handle non-finite values.
Results may differ from a plain program's by a relative error of at most 0.0063.
Values may be sent and summed in bfloat16 or wider, within the bound.
A program may use at most 64 MiB of HBM per device.

v0:
```python
import math

import jax
import jax.numpy as jnp
from jax import lax
from jax.sharding import PartitionSpec as P

HEADS = 32
HH = 8
WW = 8


def extended(block, sides, width):
    for axis, dim in sides:
        count = lax.axis_size(axis)
        forward = [(i, i + 1) for i in range(count - 1)]
        backward = [(target, source) for source, target in forward]
        low = lax.ppermute(
            lax.slice_in_dim(block, block.shape[dim] - width, None, axis=dim), axis, forward
        )
        high = lax.ppermute(lax.slice_in_dim(block, 0, width, axis=dim), axis, backward)
        block = jnp.concatenate([low, block, high], axis=dim)
    return block


def attend_heads(tensors, frames):
    query_part, key_part, value_part = tensors
    item_count, seq_len, local_heads, head_size = query_part.shape
    block_rows = min(512, seq_len)
    score_scale = 1.0 / math.sqrt(head_size)
    positions = jnp.arange(seq_len, dtype=jnp.int32) // (HH * WW)
    key_valid = positions < frames
    query_blocks = query_part.reshape(
        item_count, seq_len // block_rows, block_rows, local_heads, head_size
    )
    query_blocks = jnp.moveaxis(query_blocks, 1, 0)

    def one_block(query_block):
        scores = (
            jnp.einsum("nqhd,nkhd->nhqk", query_block, key_part, preferred_element_type=jnp.float32)
            * score_scale
        )
        scores = jnp.where(key_valid[None, None, None, :], scores, -jnp.inf)
        weights = jnp.exp(scores - jnp.max(scores, axis=3, keepdims=True))
        row_total = jnp.sum(weights, axis=3)
        rounded = weights.astype(jnp.bfloat16)
        product = jnp.einsum(
            "nhqk,nkhd->nqhd", rounded, value_part, preferred_element_type=jnp.float32
        )
        return (product / jnp.moveaxis(row_total, 1, 2)[..., None]).astype(jnp.bfloat16)

    result = lax.map(one_block, query_blocks)
    return jnp.moveaxis(result, 0, 1).reshape(item_count, seq_len, local_heads, head_size)


def adapt_input(block_out, mod_rows, down_weight):
    wide_values = block_out.astype(jnp.float32)
    centre = jnp.mean(wide_values, axis=-1, keepdims=True)
    spread = jnp.mean(jnp.square(wide_values - centre), axis=-1, keepdims=True)
    normed = (
        (wide_values - centre) * lax.rsqrt(spread + 1e-06) * (1.0 + mod_rows[1]) + mod_rows[0]
    ).astype(jnp.bfloat16)
    return jnp.einsum(
        "std,dc->stc", normed, down_weight, preferred_element_type=jnp.float32
    ).astype(jnp.bfloat16)


def body(
    hidden_state,
    queries,
    key_vectors,
    value_vectors,
    modulation,
    down_weight,
    conv_weight,
    clip_frames,
    destination,
    timestep,
):
    my_section = lax.axis_index("sec")
    my_place = lax.axis_index("ctx")
    sections, tok_rows, model_width = hidden_state.shape
    head_size = model_width // HEADS
    own_frames = clip_frames[my_section]
    my_step = timestep[my_section]

    def by_heads(tensor):
        return tensor.reshape(sections, tok_rows, HEADS, head_size)

    local_out = attend_heads(
        (
            lax.all_to_all(by_heads(queries), "ctx", split_axis=2, concat_axis=1, tiled=True),
            lax.all_to_all(by_heads(key_vectors), "ctx", split_axis=2, concat_axis=1, tiled=True),
            lax.all_to_all(by_heads(value_vectors), "ctx", split_axis=2, concat_axis=1, tiled=True),
        ),
        own_frames,
    )
    attended = lax.all_to_all(local_out, "ctx", split_axis=1, concat_axis=2, tiled=True)
    attended = attended.reshape(sections, tok_rows, model_width)
    block_out = (
        hidden_state.astype(jnp.float32) + modulation[my_step, 2] * attended.astype(jnp.float32)
    ).astype(jnp.bfloat16)
    section_ids = jnp.arange(destination.shape[0], dtype=jnp.int32)
    source = jnp.sum(jnp.where(destination == my_section, section_ids, 0))
    own_projected = adapt_input(block_out, modulation[my_step], down_weight)
    gathered = lax.all_gather(own_projected, "sec", axis=0, tiled=True)
    first_row = jnp.int32(0)
    piece_rows = gathered.shape[0]
    offset = jnp.clip(source, 0, piece_rows - 1)
    chosen = lax.dynamic_index_in_dim(gathered, offset, 0, keepdims=True)
    inside = (source >= first_row) & (source < first_row + piece_rows)
    projected = jnp.where(inside, chosen, jnp.zeros_like(own_projected))
    frames_here = tok_rows // (HH * WW)
    frame_number = my_place * frames_here + jnp.arange(frames_here, dtype=jnp.int32)
    keep_frame = (frame_number < clip_frames[source])[None, :, None, None, None]
    clip_cells = jnp.where(keep_frame, projected.reshape(sections, frames_here, HH, WW, -1), 0)
    padded = extended(clip_cells, (("ctx", 1),), 1)
    convolved = lax.conv_general_dilated(
        padded,
        conv_weight,
        (1, 1, 1),
        ((0, 0), (1, 1), (1, 1)),
        dimension_numbers=("NDHWC", "DHWIO", "NDHWC"),
        preferred_element_type=jnp.float32,
    )
    upsampled = jnp.where(keep_frame, clip_cells.astype(jnp.float32) + convolved, 0.0).astype(
        jnp.bfloat16
    )
    return upsampled.reshape(sections, tok_rows, -1)


def solution(mesh):
    in_specs = (
        P("sec", "ctx", None),
        P("sec", "ctx", None),
        P("sec", "ctx", None),
        P("sec", "ctx", None),
        P(),
        P(),
        P(),
        P(),
        P(),
        P(),
    )
    out_specs = P("sec", "ctx", None)
    return jax.shard_map(body, mesh=mesh, in_specs=in_specs, out_specs=out_specs, check_vma=False)
```

profile of v0, /device:TPU:1, one launch (start us, length us, event | category | flops | bytes accessed | tf_op | source)
XLA Modules:
  0.0 303.9 jit_solution(16420890058449033828)
XLA Ops:
  0.0 2.4 copy.39
  2.4 12.8 %all-to-all-start = ((bf16[1,128,32,128]{1,3,0,2:T(8,128)(2,1)}), bf16[1,128,32,128]{1,3,0,2:T(8,128)(2,1)}, u32[]{:S(2)}, u32[]{:S(2)}) async-start(bf16[1,128,32,128]{1,3,0,2:T(8,128)(2,1)} %bitcast.99), calls=%async_computation | async-start | bytes 2097152 | tf_op jit(solution)/shard_map/all_to_all | solution.py:92
  15.2 2.3 copy.42
  17.5 25.9 %all-to-all-done = bf16[1,128,32,128]{1,3,0,2:T(8,128)(2,1)} async-done(((bf16[1,128,32,128]{1,3,0,2:T(8,128)(2,1)}), bf16[1,128,32,128]{1,3,0,2:T(8,128)(2,1)}, u32[]{:S(2)}, u32[]{:S(2)}) %all-to-all-start) | async-done | bytes 1048608 | tf_op jit(solution)/shard_map/all_to_all | solution.py:92
  43.4 5.8 %all-to-all-start.1 = ((bf16[1,128,32,128]{1,3,0,2:T(8,128)(2,1)}), bf16[1,128,32,128]{1,3,0,2:T(8,128)(2,1)}, u32[]{:S(2)}, u32[]{:S(2)}) async-start(bf16[1,128,32,128]{1,3,0,2:T(8,128)(2,1)} %bitcast.98), calls=%async_computation.1 | async-start | bytes 2097152 | tf_op jit(solution)/shard_map/all_to_all | solution.py:93
  49.3 2.3 copy.45
  51.6 25.9 %all-to-all-done.1 = bf16[1,128,32,128]{1,3,0,2:T(8,128)(2,1)} async-done(((bf16[1,128,32,128]{1,3,0,2:T(8,128)(2,1)}), bf16[1,128,32,128]{1,3,0,2:T(8,128)(2,1)}, u32[]{:S(2)}, u32[]{:S(2)}) %all-to-all-start.1) | async-done | bytes 1048608 | tf_op jit(solution)/shard_map/all_to_all | solution.py:93
  77.5 5.9 %all-to-all-start.2 = ((bf16[1,128,32,128]{1,3,0,2:T(8,128)(2,1)}), bf16[1,128,32,128]{1,3,0,2:T(8,128)(2,1)}, u32[]{:S(2)}, u32[]{:S(2)}) async-start(bf16[1,128,32,128]{1,3,0,2:T(8,128)(2,1)} %bitcast.97), calls=%async_computation.2 | async-start | bytes 2097152 | tf_op jit(solution)/shard_map/all_to_all | solution.py:94
  83.3 0.6 fusion.54
  86.5 2.3 copy.41
  88.8 2.3 copy.44
  91.1 20.4 %all-to-all-done.2 = bf16[1,128,32,128]{1,3,0,2:T(8,128)(2,1)} async-done(((bf16[1,128,32,128]{1,3,0,2:T(8,128)(2,1)}), bf16[1,128,32,128]{1,3,0,2:T(8,128)(2,1)}, u32[]{:S(2)}, u32[]{:S(2)}) %all-to-all-start.2) | async-done | bytes 1048608 | tf_op jit(solution)/shard_map/all_to_all | solution.py:94
  111.5 2.3 copy.47
  113.8 63.7 %while.11 = (s32[]{:T(128)}, bf16[8,1,512,1,128]{4,2,3,1,0:T(8,128)(2,1)}, bf16[8,1,512,1,128]{4,2,3,1,0:T(8,128)(2,1)}, bf16[1,4096,1,128]{3,1,2,0:T(8,128)(2,1...) while((s32[]{:T(128)}, bf16[8,1,512,1,128]{4,2,3,1,0:T(8,128)(2,1)}, ...), condition=%wide.region_4.5_spmd.clone, body=%wide.region_1.4_spmd.clone.sunk | while | flops 1096977408 | bytes 31746172 | solution.py:52
  113.8 0.6 fusion.68
  114.4 2.7 fusion.69
  117.2 2.2 fusion.70
  119.3 2.4 fusion.71
  121.8 0.6 fusion.68
  122.4 2.7 fusion.69
  125.1 2.2 fusion.70
  127.3 2.4 fusion.71
  129.7 0.6 fusion.68
  130.4 2.7 fusion.69
  133.1 2.2 fusion.70
  135.3 2.4 fusion.71
  137.7 0.6 fusion.68
  138.3 2.7 fusion.69
  141.1 2.2 fusion.70
  143.2 2.4 fusion.71
  145.6 0.6 fusion.68
  146.3 2.7 fusion.69
  149.0 2.2 fusion.70
  151.2 2.4 fusion.71
  153.6 0.6 fusion.68
  154.2 2.7 fusion.69
  157.0 2.2 fusion.70
  159.2 2.4 fusion.71
  161.6 0.6 fusion.68
  162.2 2.7 fusion.69
  164.9 2.2 fusion.70
  167.1 2.4 fusion.71
  169.5 0.6 fusion.68
  170.2 2.7 fusion.69
  172.9 2.2 fusion.70
  175.1 2.4 fusion.71
  177.5 4.3 %copy.55 = bf16[1,4096,1,128]{3,2,0,1:T(2,128)(2,1)} copy(bf16[1,4096,1,128]{3,1,2,0:T(8,128)(2,1)} %bitcast.101) | data formatting | bytes 2097152 | tf_op jit(solution)/shard_map/reshape;transpose | solution.py:53
  182.3 24.3 %reduce.6 = bf16[4096,128]{1,0:T(8,128)(2,1)} reduce(bf16[4096,1,1,128]{3,2,1,0:T(2,128)(2,1)} %bitcast.95, bf16[]{:T(256)} %broadcast.118), dimensions={1,2}, to_apply=%bitcast.83.reduce_sub_computation | reduce | bytes 2097154
  206.7 2.1 reshape.170
  208.8 5.9 %all-to-all-start.3 = ((bf16[32,2,8192]{2,1,0:T(2,128)(2,1)}), bf16[32,2,8192]{2,1,0:T(2,128)(2,1)}, u32[]{:S(2)}, u32[]{:S(2)}) async-start(bf16[32,2,8192]{2,1,0:T(2,128)(2,1)} %reshape.170), calls=%async_computation.3 | async-start | bytes 2097152 | tf_op jit(solution)/shard_map/all_to_all | solution.py:98
  219.2 1.1 add_compare_fusion
  220.2 1.7 dynamic-slice_add_fusion
  221.9 20.8 %all-to-all-done.3 = bf16[32,2,8192]{2,1,0:T(2,128)(2,1)} async-done(((bf16[32,2,8192]{2,1,0:T(2,128)(2,1)}), bf16[32,2,8192]{2,1,0:T(2,128)(2,1)}, u32[]{:S(2)}, u32[]{:S(2)}) %all-to-all-start.3) | async-done | bytes 1048608 | tf_op jit(solution)/shard_map/all_to_all | solution.py:98
  242.7 5.8 %reshape.171 = bf16[4096,1,1,128]{3,2,1,0:T(2,128)(2,1)} reshape(bf16[32,2,8192]{2,1,0:T(2,128)(2,1)} %all-to-all-done.3) | data formatting | bytes 2097152
  248.4 3.8 %bitcast_convert_fusion = f32[1,4096,1,128]{3,2,0,1:T(1,128)S(1)} fusion(bf16[4096,1,1,128]{3,2,1,0:T(2,128)(2,1)} %reshape.171), kind=kLoop, calls=%fused_computation.65 | loop fusion | flops 524288 | bytes 3145728 | tf_op jit(solution)/shard_map/convert_element_type | solution.py:101
  252.2 2.6 copy.50
  254.8 2.7 reshape.164
  257.5 2.4 convert_reduce_fusion
  261.0 23.3 %all-gather = bf16[1024,256]{1,0:T(8,128)(2,1)S(1)} all-gather(bf16[128,256]{1,0:T(8,128)(2,1)S(1)} %convolution_convert_fusion), channel_id=2, replica_groups=mesh['sec'=8,'ctx'=32] {'sec'}, dimensions={0}, use_global_device_ids=true | all-gather | bytes 589824 | tf_op jit(solution)/shard_map/all_gather | solution.py:106
  284.6 9.2 %collective-permute-start.1 = (bf16[1,1,8,8,256]{4,0,3,2,1:T(2,128)(2,1)S(1)}, bf16[1,1,8,8,256]{4,0,3,2,1:T(2,128)(2,1)S(1)}, u32[]{:S(2)}, u32[]{:S(2)}) collective-permute-start(bf16[1,1,8,8,256]{4,0,3,2,1:T(2,128)(2,1)S(1)} %get-tuple-element.97), channel_id=1, source_target_pairs={{1,0},{2,1},{3,2},{4,3},{5,4},{6,5},{7,6},{8,7},{9,8},{10,9},{11,1... | collective-permute-start | bytes 98312 | tf_op jit(solution)/shard_map/ppermute | solution.py:21
  293.8 4.8 %collective-permute-start = (bf16[1,1,8,8,256]{4,0,3,2,1:T(2,128)(2,1)S(1)}, bf16[1,1,8,8,256]{4,0,3,2,1:T(2,128)(2,1)S(1)}, u32[]{:S(2)}, u32[]{:S(2)}) collective-permute-start(bf16[1,1,8,8,256]{4,0,3,2,1:T(2,128)(2,1)S(1)} %get-tuple-element.96), channel_id=1, source_target_pairs={{0,1},{1,2},{2,3},{3,4},{4,5},{5,6},{6,7},{7,8},{8,9},{9,10},{10,1... | collective-permute-start | bytes 98312 | tf_op jit(solution)/shard_map/ppermute | solution.py:18
  298.7 1.3 collective-permute-done
  300.0 3.2 %fusion.42 = bf16[1,2,8,8,256]{4,0,3,2,1:T(2,128)(2,1)S(1)} fusion(bf16[3,3,3,256,256]{4,3,2,1,0:T(8,128)(2,1)S(1)} %copy-done, bf16[1,1,8,8,256]{4,0,3,2,1:T(2,128)(2,1)S(1)} %collective-permute-done.1, bf16[1,2,8,8,256]{4,0,3,2,1:T(2,128)(2,1)S(1)} %broadcast_select_fusion, bf16[1,1,8,8,256]{4,0,3,2,1:T(2,128)(2,1)S(1)} %collective-permute-done, ...), kind=kOutput, calls=%fused_computation.40 | convolution fusion | flops 381157376 | bytes 3735554 | tf_op jit(solution)/shard_map/conv_general_dilated | solution.py:118
  303.2 0.6 copy.52
  (44 shorter events, 3.1 us)
Async XLA Ops:
  0.0 300.0 %copy-start = (bf16[3,3,3,256,256]{4,3,2,1,0:T(8,128)(2,1)S(1)}, bf16[3,3,3,256,256]{4,3,2,1,0:T(8,128)(2,1)}, u32[]{:S(2)}) copy-start(bf16[3,3,3,256,256]{4,3,2,1,0:T(8,128)(2,1)} %param.18) | copy-start | bytes 10616836
  2.4 41.0 %all-to-all-start = ((bf16[1,128,32,128]{1,3,0,2:T(8,128)(2,1)}), bf16[1,128,32,128]{1,3,0,2:T(8,128)(2,1)}, u32[]{:S(2)}, u32[]{:S(2)}) async-start(bf16[1,128,32,128]{1,3,0,2:T(8,128)(2,1)} %bitcast.99), calls=%async_computation | async-start | bytes 2097152 | tf_op jit(solution)/shard_map/all_to_all | solution.py:92
  43.4 34.0 %all-to-all-start.1 = ((bf16[1,128,32,128]{1,3,0,2:T(8,128)(2,1)}), bf16[1,128,32,128]{1,3,0,2:T(8,128)(2,1)}, u32[]{:S(2)}, u32[]{:S(2)}) async-start(bf16[1,128,32,128]{1,3,0,2:T(8,128)(2,1)} %bitcast.98), calls=%async_computation.1 | async-start | bytes 2097152 | tf_op jit(solution)/shard_map/all_to_all | solution.py:93
  49.3 34.0 %copy-start.7 = (s32[8]{0:T(128)S(1)}, s32[8]{0:T(128)}, u32[]{:S(2)}) copy-start(s32[8]{0:T(128)} %param.20) | copy-start | bytes 100
  49.3 36.6 %copy-start.4 = (s32[8]{0:T(128)S(1)}, s32[8]{0:T(128)}, u32[]{:S(2)}) copy-start(s32[8]{0:T(128)} %param.19) | copy-start | bytes 100
  77.5 34.0 %all-to-all-start.2 = ((bf16[1,128,32,128]{1,3,0,2:T(8,128)(2,1)}), bf16[1,128,32,128]{1,3,0,2:T(8,128)(2,1)}, u32[]{:S(2)}, u32[]{:S(2)}) async-start(bf16[1,128,32,128]{1,3,0,2:T(8,128)(2,1)} %bitcast.97), calls=%async_computation.2 | async-start | bytes 2097152 | tf_op jit(solution)/shard_map/all_to_all | solution.py:94
  117.2 2.2 copy-start.1
  125.1 2.2 copy-start.1
  133.1 2.2 copy-start.1
  141.1 2.2 copy-start.1
  149.0 2.2 copy-start.1
  157.0 2.2 copy-start.1
  164.9 2.2 copy-start.1
  172.9 2.2 copy-start.1
  206.7 10.0 %copy-start.8 = (s32[8]{0:T(128)S(1)}, s32[8]{0:T(128)}, u32[]{:S(2)}) copy-start(s32[8]{0:T(128)} %param.21) | copy-start | bytes 100
  208.8 33.9 %all-to-all-start.3 = ((bf16[32,2,8192]{2,1,0:T(2,128)(2,1)}), bf16[32,2,8192]{2,1,0:T(2,128)(2,1)}, u32[]{:S(2)}, u32[]{:S(2)}) async-start(bf16[32,2,8192]{2,1,0:T(2,128)(2,1)} %reshape.170), calls=%async_computation.3 | async-start | bytes 2097152 | tf_op jit(solution)/shard_map/all_to_all | solution.py:98
  257.5 2.9 copy-start.2
  257.5 2.9 copy-start.3
  257.5 2.9 copy-start.6
  260.4 23.9 %copy-start.5 = (pred[2]{0:T(512)(128)(4,1)S(1)}, pred[2]{0:T(512)(128)(4,1)}, u32[]{:S(2)}) copy-start(pred[2]{0:T(512)(128)(4,1)} %add_compare_fusion) | copy-start | bytes 10
  284.6 14.0 %collective-permute-start.1 = (bf16[1,1,8,8,256]{4,0,3,2,1:T(2,128)(2,1)S(1)}, bf16[1,1,8,8,256]{4,0,3,2,1:T(2,128)(2,1)S(1)}, u32[]{:S(2)}, u32[]{:S(2)}) collective-permute-start(bf16[1,1,8,8,256]{4,0,3,2,1:T(2,128)(2,1)S(1)} %get-tuple-element.97), channel_id=1, source_target_pairs={{1,0},{2,1},{3,2},{4,3},{5,4},{6,5},{7,6},{8,7},{9,8},{10,9},{11,1... | collective-permute-start | bytes 98312 | tf_op jit(solution)/shard_map/ppermute | solution.py:21
  293.8 6.2 %collective-permute-start = (bf16[1,1,8,8,256]{4,0,3,2,1:T(2,128)(2,1)S(1)}, bf16[1,1,8,8,256]{4,0,3,2,1:T(2,128)(2,1)S(1)}, u32[]{:S(2)}, u32[]{:S(2)}) collective-permute-start(bf16[1,1,8,8,256]{4,0,3,2,1:T(2,128)(2,1)S(1)} %get-tuple-element.96), channel_id=1, source_target_pairs={{0,1},{1,2},{2,3},{3,4},{4,5},{5,6},{6,7},{7,8},{8,9},{9,10},{10,1... | collective-permute-start | bytes 98312 | tf_op jit(solution)/shard_map/ppermute | solution.py:18
where the time goes:
time: 305 us; the launch traced here: 304 us
  waiting for transfers between devices  94.3 us (31%)
  other arithmetic  56.8 us (19%)
  matrix products  45.1 us (15%)
  starting transfers between devices  44.4 us (15%)
  local copies, waits for them, and re-layouts  33.8 us (11%)
  blocking collectives  23.3 us (8%)
  between operations  6.06 us (2%)
    all_to_all x1, waiting for transfers between devices, body(): lax.all_to_all(by_heads(queries), 'ctx', split_axis=2, concat_axis=1, til...  25.9 us
    all_to_all x1, waiting for transfers between devices, body(): lax.all_to_all(by_heads(key_vectors), 'ctx', split_axis=2, concat_axis=1,...  25.9 us
    unnamed x1, other arithmetic  24.3 us
    all_gather x1, blocking collectives, body(): gathered = lax.all_gather(own_projected, 'sec', axis=0, tiled=True)  23.3 us
    dot_general x8, matrix products, one_block(): jnp.einsum('nqhd,nkhd->nhqk', query_block, key_part, preferred_element_ty...  22 us
    all_to_all x1, waiting for transfers between devices, body(): lax.all_to_all(local_out, 'ctx', split_axis=1, concat_axis=2, tiled=True)  20.8 us
    all_to_all x1, waiting for transfers between devices, body(): lax.all_to_all(by_heads(value_vectors), 'ctx', split_axis=2, concat_axis=...  20.4 us
    dot_general x8, matrix products, one_block(): jnp.einsum('nhqk,nkhd->nqhd', rounded, value_part, preferred_element_type...  19.3 us
  transfers between devices with their start and end apart: 6, of which 5 were waited for; matrix products, arithmetic and copies ran while one was open for 4% of the time, Pallas kernels for 0%

commit v1 on v0

v1 whole, which is shorter than its diff:
```python
import functools
import math

import jax
import jax.numpy as jnp
from jax import lax
from jax.experimental import pallas as pl
from jax.experimental.pallas import tpu as pltpu
from jax.sharding import PartitionSpec as P

HEADS = 32
HD = 128
CELLS = 64
MESH = pl.DeviceIdType.MESH
BF = jnp.bfloat16
F32 = jnp.float32


def kernel(
    frames_ref, dest_ref, step_ref,
    q_hbm, k_hbm, v_hbm, hid_hbm, mod_hbm, down_hbm, conv_hbm,
    out_ref,
    qf, kf, vf, k2, v2, o_send, att, hid, mod, down, conv, proj, xpad, lohalo, hihalo, upbuf, gathered,
    send_k, send_v, send_q, send_o, send_h, send_g,
    recv_k, recv_v, recv_q, recv_o, recv_h, recv_g, w_sem,
):
    rows = q_hbm.shape[0]
    ctx = lax.axis_size("ctx")
    secs = lax.axis_size("sec")
    me = lax.axis_index("ctx")
    sec = lax.axis_index("sec")
    zi, yi, ci = me // 4, (me // 2) % 2, me % 2
    group = 4 * rows
    groups = ctx // 4

    def place(dz, dy, dc):
        return lax.rem(zi + dz, groups) * 4 + lax.rem(yi + dy, 2) * 2 + lax.rem(ci + dc, 2)

    barrier = pltpu.get_barrier_semaphore()

    def greet_ctx(i, carry):
        pl.semaphore_signal(barrier, inc=1, device_id={"ctx": lax.rem(me + i, ctx)}, device_id_type=MESH)
        return carry

    def greet_sec(i, carry):
        pl.semaphore_signal(barrier, inc=1, device_id={"sec": lax.rem(sec + i, secs)}, device_id_type=MESH)
        return carry

    lax.fori_loop(1, ctx, greet_ctx, 0)
    lax.fori_loop(1, secs, greet_sec, 0)
    pl.semaphore_wait(barrier, ctx - 1 + secs - 1)

    my_rows = pl.ds(pl.multiple_of(me * rows, rows), rows)
    my_cols = pl.ds(pl.multiple_of(me * HD, HD), HD)

    def scatter(src, dst, send, recv):
        def one(i, carry):
            k = i // 4
            dz = lax.rem(jnp.where(k % 2 == 0, k // 2 + 1, 7 - k // 2), 8)
            dz = jnp.where(k == 7, 0, dz)
            j = 3 - i % 4
            to = place(dz, j // 2, j % 2)
            cols = pl.ds(pl.multiple_of(to * HD, HD), HD)
            pltpu.make_async_remote_copy(
                src_ref=src.at[:, cols], dst_ref=dst.at[my_rows], send_sem=send, recv_sem=recv,
                device_id={"ctx": to}, device_id_type=MESH,
            ).start()
            return carry

        lax.fori_loop(0, ctx - 1, one, 0)
        pltpu.make_async_copy(src.at[:, my_cols], dst.at[my_rows], recv).start()

    scatter(k_hbm, kf, send_k, recv_k)
    scatter(v_hbm, vf, send_v, recv_v)
    scatter(q_hbm, qf, send_q, recv_q.at[zi])
    loads = [
        pltpu.make_async_copy(a, b, w_sem.at[n])
        for n, (a, b) in enumerate(((hid_hbm, hid), (mod_hbm, mod), (down_hbm, down), (conv_hbm, conv)))
    ]
    for load in loads:
        load.start()

    frames = frames_ref[sec]
    pltpu.make_async_copy(kf, kf, recv_k).wait()
    first = kf[0:1, :]
    key_at = lax.broadcasted_iota(jnp.int32, kf.shape, 0)
    valid = key_at < frames * CELLS
    kk = jnp.where(valid, kf[...].astype(F32), first.astype(F32)).astype(BF)
    k2[:, 0:HD] = kk
    k2[:, HD:] = kk
    pltpu.make_async_copy(vf, vf, recv_v).wait()
    v2[:, 0:HD] = jnp.where(valid, vf[...].astype(F32), 0.0).astype(BF)
    v2[:, HD:] = jnp.where(valid, 1.0, 0.0).astype(BF)

    scale = math.log2(math.e) / math.sqrt(HD)

    def attend(k, carry):
        dz = lax.rem(jnp.where(k % 2 == 0, 4 - k // 2, 5 + k // 2), groups)
        g = lax.rem(zi + dz, groups)
        at = pl.ds(pl.multiple_of(g * group, group), group)
        pltpu.make_async_copy(qf.at[at], qf.at[at], recv_q.at[g]).wait()
        wide = qf[at, :].astype(F32) * scale
        high = wide.astype(BF)
        low = (wide - high.astype(F32)).astype(BF)
        q2 = jnp.concatenate([high, low], axis=1)
        scores = lax.dot_general(q2, k2[...], (((1,), (1,)), ((), ())), preferred_element_type=F32)
        top = jnp.max(scores, axis=1, keepdims=True)
        weights = jnp.exp2(scores - top).astype(BF)
        both = jnp.dot(weights, v2[...], preferred_element_type=F32)
        o_send[at, :] = (both[:, 0:HD] / both[:, HD:]).astype(BF)
        for j in (3, 2, 1, 0):
            to = place(dz, j // 2, j % 2)
            block = o_send.at[pl.ds(pl.multiple_of(to * rows, rows), rows)]

            def remote(to=to, block=block):
                pltpu.make_async_remote_copy(
                    src_ref=block, dst_ref=att.at[:, my_cols], send_sem=send_o, recv_sem=recv_o,
                    device_id={"ctx": to}, device_id_type=MESH,
                ).start()

            if j:
                remote()
            else:
                pl.when(k < groups - 1)(remote)
        return carry

    lax.fori_loop(0, groups, attend, 0)
    pltpu.make_async_copy(o_send.at[my_rows], att.at[:, my_cols], recv_o).start()

    for load in loads:
        load.wait()
    now = step_ref[sec]
    shift, scale_up, gate = (mod[n, pl.ds(now, 1), :] for n in range(3))
    pltpu.make_async_copy(att, att, recv_o).wait()
    block = (hid[...].astype(F32) + gate * att[...].astype(F32)).astype(BF)
    wide = block.astype(F32)
    centre = jnp.mean(wide, axis=1, keepdims=True)
    away = wide - centre
    spread = jnp.mean(away * away, axis=1, keepdims=True)
    normed = (away * lax.rsqrt(spread + 1e-06) * (1.0 + scale_up) + shift).astype(BF)
    projected = jnp.dot(normed, down[...], preferred_element_type=F32).astype(BF)
    cell = me * rows + lax.broadcasted_iota(jnp.int32, projected.shape, 0)
    keep = cell < frames * CELLS
    clip = jnp.where(keep, projected.astype(F32), 0.0)
    proj[...] = clip.astype(BF)

    below = lax.rem(me + ctx - 1, ctx)
    above = lax.rem(me + 1, ctx)
    up = pltpu.make_async_remote_copy(
        src_ref=proj.at[pl.ds(rows - CELLS, CELLS)], dst_ref=lohalo, send_sem=send_h.at[0], recv_sem=recv_h.at[0],
        device_id={"ctx": above}, device_id_type=MESH)
    dn = pltpu.make_async_remote_copy(
        src_ref=proj.at[pl.ds(0, CELLS)], dst_ref=hihalo, send_sem=send_h.at[1], recv_sem=recv_h.at[1],
        device_id={"ctx": below}, device_id_type=MESH)
    up.start()
    dn.start()
    up.wait_recv()
    dn.wait_recv()

    total_rows = rows + 2 * CELLS
    xpad[0:CELLS, :] = jnp.where(me > 0, lohalo[...].astype(F32), 0.0)
    xpad[CELLS:CELLS + rows, :] = clip
    xpad[CELLS + rows:, :] = jnp.where(me < ctx - 1, hihalo[...].astype(F32), 0.0)
    padded = xpad[...]
    at = lax.broadcasted_iota(jnp.int32, padded.shape, 0) % CELLS
    row, col = at // 8, at % 8
    total = clip
    for b in range(3):
        for e in range(3):
            step = (b - 1) * 8 + (e - 1)
            moved = padded if step == 0 else pltpu.roll(padded, (-step) % total_rows, 0)
            inside = (row + b - 1 >= 0) & (row + b - 1 < 8) & (col + e - 1 >= 0) & (col + e - 1 < 8)
            moved = jnp.where(inside, moved, 0.0).astype(BF)
            for a in range(3):
                total += jnp.dot(moved[a * CELLS:a * CELLS + rows], conv[a * 9 + b * 3 + e], preferred_element_type=F32)
    upbuf[...] = jnp.where(keep, total, 0.0).astype(BF)

    def spread_out(i, carry):
        pltpu.make_async_remote_copy(
            src_ref=upbuf, dst_ref=gathered.at[sec], send_sem=send_g, recv_sem=recv_g,
            device_id={"sec": lax.rem(sec + i, secs)}, device_id_type=MESH,
        ).start()
        return carry

    lax.fori_loop(1, secs, spread_out, 0)
    pltpu.make_async_copy(upbuf, gathered.at[sec], recv_g).start()

    source = jnp.int32(0)
    for s in range(dest_ref.shape[0]):
        source = jnp.where(dest_ref[s] == sec, s, source)
    others = pl.ds(0, (ctx - 1) * rows)
    pltpu.make_async_copy(kf.at[others], kf.at[others], send_k).wait()
    pltpu.make_async_copy(vf.at[others], vf.at[others], send_v).wait()
    pltpu.make_async_copy(qf.at[others], qf.at[others], send_q).wait()
    pltpu.make_async_copy(o_send.at[others], o_send.at[others], send_o).wait()
    up.wait_send()
    dn.wait_send()
    sent = pl.ds(0, secs - 1)
    pltpu.make_async_copy(gathered.at[sent], gathered.at[sent], send_g).wait()
    pltpu.make_async_copy(gathered, gathered, recv_g).wait()
    out_ref[...] = gathered[source]


def body(hidden, queries, keys, values, modulation, down_weight, conv_weight, clip_frames, destination, timestep):
    _, rows, width = queries.shape
    seq = rows * lax.axis_size("ctx")
    secs = lax.axis_size("sec")
    groups = lax.axis_size("ctx") // 4
    up = down_weight.shape[1]
    flat = lambda t: t.reshape(rows, width)
    smem = pl.BlockSpec(memory_space=pltpu.SMEM)
    anywhere = pl.BlockSpec(memory_space=pl.ANY)
    dma = pltpu.SemaphoreType.DMA
    taps = conv_weight.reshape(27, up, up)
    modulation = jnp.swapaxes(modulation, 0, 1)
    out = pl.pallas_call(
        kernel,
        out_shape=jax.ShapeDtypeStruct((rows, up), BF),
        in_specs=[smem] * 3 + [anywhere] * 7,
        out_specs=pl.BlockSpec(memory_space=pltpu.VMEM),
        scratch_shapes=[
            pltpu.VMEM((seq, HD), BF), pltpu.VMEM((seq, HD), BF), pltpu.VMEM((seq, HD), BF),
            pltpu.VMEM((seq, 2 * HD), BF), pltpu.VMEM((seq, 2 * HD), BF),
            pltpu.VMEM((seq, HD), BF), pltpu.VMEM((rows, width), BF), pltpu.VMEM((rows, width), BF),
            pltpu.VMEM(modulation.shape, F32), pltpu.VMEM(down_weight.shape, BF), pltpu.VMEM(taps.shape, BF),
            pltpu.VMEM((rows, up), BF), pltpu.VMEM((rows + 2 * CELLS, up), F32),
            pltpu.VMEM((CELLS, up), BF), pltpu.VMEM((CELLS, up), BF),
            pltpu.VMEM((rows, up), BF), pltpu.VMEM((secs, rows, up), BF),
            dma, dma, dma, dma, dma((2,)), dma,
            dma, dma, dma((groups,)), dma, dma((2,)), dma, dma((4,)),
        ],
        compiler_params=pltpu.CompilerParams(
            collective_id=0, has_side_effects=True, vmem_limit_bytes=60 << 20
        ),
        name="section_kernel",
    )(clip_frames, destination, timestep, flat(queries), flat(keys), flat(values), flat(hidden), modulation, down_weight, taps)
    return out.reshape(1, rows, up)


def solution(mesh):
    tokens = P("sec", "ctx", None)
    return jax.shard_map(
        body, mesh=mesh, in_specs=(tokens,) * 4 + (P(),) * 6, out_specs=tokens, check_vma=False
    )
```

time: 305 us -> 138 us (0.45)
  Pallas kernels: 0 us -> 134 us
  waiting for transfers between devices: 94.3 us -> 0 us
  other arithmetic: 56.8 us -> 0 us
  matrix products: 45.1 us -> 0 us
  starting transfers between devices: 44.4 us -> 0 us
  local copies, waits for them, and re-layouts: 33.8 us -> 1.47 us
  blocking collectives: 23.3 us -> 0 us
  between operations: 6.06 us -> 0.01 us
    pallas_call x0 -> x1, Pallas kernels: none -> 134 us  [body(): pl.pallas_call(kernel, out_shape=jax.ShapeDtypeStruct((rows, up), BF), in...]
    all_to_all x4 -> x0, waiting for transfers between devices: 93 us -> none  [the longest x1 25.9 us: body(): lax.all_to_all(by_heads(queries), 'ctx', split_axis=2, concat_axis=1, til...]
    dot_general x17 -> x0, matrix products: 41.9 us -> none  [the longest x8 22 us: one_block(): jnp.einsum('nqhd,nkhd->nhqk', query_block, key_part, preferred_element_ty...]
    all_to_all x4 -> x0, starting transfers between devices: 30.4 us -> none  [the longest x1 12.8 us: body(): lax.all_to_all(by_heads(queries), 'ctx', split_axis=2, concat_axis=1, til...]
    unnamed x1 -> x0, other arithmetic: 24.3 us -> none
    all_gather x1 -> x0, blocking collectives: 23.3 us -> none  [body(): gathered = lax.all_gather(own_projected, 'sec', axis=0, tiled=True)]
    reduce_sum x11 -> x0, other arithmetic: 20.7 us -> none  [the longest x8 17.3 us: one_block(): row_total = jnp.sum(weights, axis=3)]
    unnamed x23 -> x1, local copies, waits for them, and re-layouts: 16 us -> 1.47 us
  transfers between devices with their start and end apart: 6 -> 0, of which waited for: 5 -> 0; matrix products, arithmetic and copies ran while one was open for 4% -> 0% of each run, Pallas kernels for 0% -> 0%
where the time goes in v1:
time: 138 us; the launch traced here: 136 us
  Pallas kernels  134 us (97%)
  local copies, waits for them, and re-layouts  1.47 us (1%)
    pallas_call x1, Pallas kernels, body(): pl.pallas_call(kernel, out_shape=jax.ShapeDtypeStruct((rows, up), BF), in...  134 us

profile of v1, /device:TPU:1, one launch (start us, length us, event | category | flops | bytes accessed | tf_op | source)
XLA Modules:
  0.0 135.9 jit_solution(4490062359785741337)
XLA Ops:
  0.0 134.4 %section_kernel.1 = bf16[128,256]{1,0:T(8,128)(2,1)} custom-call(s32[8]{0:T(128)} %frames_ref.1, s32[8]{0:T(128)} %dest_ref.1, s32[8]{0:T(128)} %step_ref.1, bf16[128,4096]{1,0:T(8,128)(2,1)} %bitcast.9, bf16[128,4096]{1,0:T(8,128)(2,1)} %bitcast.10, bf16[128,4096]{1,0:T(8,128)(2,1)} %bitcast.11, bf16[128,4096]{1,0:T(8,128)(2,1)} %bitcast.12, ...), custom_call_target="tpu_custom_call" | custom-call | tf_op jit(solution)/shard_map/section_kernel/pallas_call | solution.py:216
  134.4 1.5 %copy.12 = bf16[1,128,256]{2,1,0:T(8,128)(2,1)} copy(bf16[1,128,256]{2,1,0:T(8,128)(2,1)} %bitcast.13) | data formatting | bytes 131072

commit v2 on v1

--- a/solution.py
+++ b/solution.py
@@ -11,6 +11,7 @@
 HEADS = 32
 HD = 128
 CELLS = 64
+SUB = 256
 MESH = pl.DeviceIdType.MESH
 BF = jnp.bfloat16
 F32 = jnp.float32
@@ -20,7 +21,7 @@
     frames_ref, dest_ref, step_ref,
     q_hbm, k_hbm, v_hbm, hid_hbm, mod_hbm, down_hbm, conv_hbm,
     out_ref,
-    qf, kf, vf, k2, v2, o_send, att, hid, mod, down, conv, proj, xpad, lohalo, hihalo, upbuf, gathered,
+    qf, kf, vf, k2, v2, o_send, att, hid, mod, down, conv, proj, xpad, lohalo, hihalo, upbuf, gathered, scores,
     send_k, send_v, send_q, send_o, send_h, send_g,
     recv_k, recv_v, recv_q, recv_o, recv_h, recv_g, w_sem,
 ):
@@ -50,15 +51,16 @@
     lax.fori_loop(1, secs, greet_sec, 0)
     pl.semaphore_wait(barrier, ctx - 1 + secs - 1)
 
+    def offset(k):
+        half = groups // 2
+        return lax.rem(jnp.where(k % 2 == 0, half - k // 2, half + 1 + k // 2), groups)
+
     my_rows = pl.ds(pl.multiple_of(me * rows, rows), rows)
     my_cols = pl.ds(pl.multiple_of(me * HD, HD), HD)
 
     def scatter(src, dst, send, recv):
         def one(i, carry):
-            k = i // 4
-            dz = lax.rem(jnp.where(k % 2 == 0, k // 2 + 1, 7 - k // 2), 8)
-            dz = jnp.where(k == 7, 0, dz)
-            j = 3 - i % 4
+            dz, j = lax.rem(groups - offset(i // 4), groups), 3 - i % 4
             to = place(dz, j // 2, j % 2)
             cols = pl.ds(pl.multiple_of(to * HD, HD), HD)
             pltpu.make_async_remote_copy(
@@ -95,19 +97,32 @@
     scale = math.log2(math.e) / math.sqrt(HD)
 
     def attend(k, carry):
-        dz = lax.rem(jnp.where(k % 2 == 0, 4 - k // 2, 5 + k // 2), groups)
+        dz = offset(k)
         g = lax.rem(zi + dz, groups)
         at = pl.ds(pl.multiple_of(g * group, group), group)
         pltpu.make_async_copy(qf.at[at], qf.at[at], recv_q.at[g]).wait()
-        wide = qf[at, :].astype(F32) * scale
-        high = wide.astype(BF)
-        low = (wide - high.astype(F32)).astype(BF)
-        q2 = jnp.concatenate([high, low], axis=1)
-        scores = lax.dot_general(q2, k2[...], (((1,), (1,)), ((), ())), preferred_element_type=F32)
-        top = jnp.max(scores, axis=1, keepdims=True)
-        weights = jnp.exp2(scores - top).astype(BF)
-        both = jnp.dot(weights, v2[...], preferred_element_type=F32)
-        o_send[at, :] = (both[:, 0:HD] / both[:, HD:]).astype(BF)
+        start = g * group
+
+        def part(i):
+            return pl.ds(pl.multiple_of(start + i * SUB, SUB), SUB)
+
+        def score(i):
+            wide = qf[part(i), :].astype(F32) * scale
+            high = wide.astype(BF)
+            low = (wide - high.astype(F32)).astype(BF)
+            q2 = jnp.concatenate([high, low], axis=1)
+            return lax.dot_general(q2, k2[...], (((1,), (1,)), ((), ())), preferred_element_type=F32)
+
+        parts = group // SUB
+        scores[0] = score(0)
+        for i in range(parts):
+            if i + 1 < parts:
+                scores[(i + 1) % 2] = score(i + 1)
+            here = scores[i % 2]
+            top = jnp.max(here, axis=1, keepdims=True)
+            weights = jnp.exp2(here - top).astype(BF)
+            both = jnp.dot(weights, v2[...], preferred_element_type=F32)
+            o_send[part(i), :] = (both[:, 0:HD] / both[:, HD:]).astype(BF)
         for j in (3, 2, 1, 0):
             to = place(dz, j // 2, j % 2)
             block = o_send.at[pl.ds(pl.multiple_of(to * rows, rows), rows)]
@@ -226,6 +241,7 @@
             pltpu.VMEM((rows, up), BF), pltpu.VMEM((rows + 2 * CELLS, up), F32),
             pltpu.VMEM((CELLS, up), BF), pltpu.VMEM((CELLS, up), BF),
             pltpu.VMEM((rows, up), BF), pltpu.VMEM((secs, rows, up), BF),
+            pltpu.VMEM((2, SUB, seq), F32),
             dma, dma, dma, dma, dma((2,)), dma,
             dma, dma, dma((groups,)), dma, dma((2,)), dma, dma((4,)),
         ],

time: 138 us -> 121 us (0.88); the launches traced: 136 us -> 120 us
  Pallas kernels: 134 us -> 119 us
    pallas_call x1, Pallas kernels: 134 us -> 119 us  [body(): pl.pallas_call(kernel, out_shape=jax.ShapeDtypeStruct((rows, up), BF), in...]
where the time goes in v2:
time: 121 us; the launch traced here: 120 us
  Pallas kernels  119 us (98%)
  local copies, waits for them, and re-layouts  1.47 us (1%)
    pallas_call x1, Pallas kernels, body(): pl.pallas_call(kernel, out_shape=jax.ShapeDtypeStruct((rows, up), BF), in...  119 us

profile of v2, /device:TPU:1, one launch (start us, length us, event | category | flops | bytes accessed | tf_op | source)
XLA Modules:
  0.0 120.5 jit_solution(14384061368063658349)
XLA Ops:
  0.0 119.0 %section_kernel.1 = bf16[128,256]{1,0:T(8,128)(2,1)} custom-call(s32[8]{0:T(128)} %frames_ref.1, s32[8]{0:T(128)} %dest_ref.1, s32[8]{0:T(128)} %step_ref.1, bf16[128,4096]{1,0:T(8,128)(2,1)} %bitcast.9, bf16[128,4096]{1,0:T(8,128)(2,1)} %bitcast.10, bf16[128,4096]{1,0:T(8,128)(2,1)} %bitcast.11, bf16[128,4096]{1,0:T(8,128)(2,1)} %bitcast.12, ...), custom_call_target="tpu_custom_call" | custom-call | tf_op jit(solution)/shard_map/section_kernel/pallas_call | solution.py:231
  119.0 1.5 %copy.12 = bf16[1,128,256]{2,1,0:T(8,128)(2,1)} copy(bf16[1,128,256]{2,1,0:T(8,128)(2,1)} %bitcast.13) | data formatting | bytes 131072

commit v3 on v2

--- a/solution.py
+++ b/solution.py
@@ -12,6 +12,7 @@
 HD = 128
 CELLS = 64
 SUB = 256
+LATE = 32
 MESH = pl.DeviceIdType.MESH
 BF = jnp.bfloat16
 F32 = jnp.float32
@@ -21,7 +22,7 @@
     frames_ref, dest_ref, step_ref,
     q_hbm, k_hbm, v_hbm, hid_hbm, mod_hbm, down_hbm, conv_hbm,
     out_ref,
-    qf, kf, vf, k2, v2, o_send, att, hid, mod, down, conv, proj, xpad, lohalo, hihalo, upbuf, gathered, scores,
+    qf, kf, vf, k2, v2, o_send, att, hid, mod, down, conv, proj, xpad, lohalo, hihalo, last_halo, clip_own, gathered_0, gathered_1, scores,
     send_k, send_v, send_q, send_o, send_h, send_g,
     recv_k, recv_v, recv_q, recv_o, recv_h, recv_g, w_sem,
 ):
@@ -30,7 +31,11 @@
     secs = lax.axis_size("sec")
     me = lax.axis_index("ctx")
     sec = lax.axis_index("sec")
+    below = lax.rem(me + ctx - 1, ctx)
+    above = lax.rem(me + 1, ctx)
     zi, yi, ci = me // 4, (me // 2) % 2, me % 2
+    parts = ((0, rows - LATE), (rows - LATE, LATE))
+    last = len(parts) - 1
     group = 4 * rows
     groups = ctx // 4
 
@@ -44,12 +49,14 @@
         return carry
 
     def greet_sec(i, carry):
-        pl.semaphore_signal(barrier, inc=1, device_id={"sec": lax.rem(sec + i, secs)}, device_id_type=MESH)
+        for place_at in (me, above, below):
+            pl.semaphore_signal(
+                barrier, inc=1, device_id={"sec": lax.rem(sec + i, secs), "ctx": place_at}, device_id_type=MESH)
         return carry
 
     lax.fori_loop(1, ctx, greet_ctx, 0)
     lax.fori_loop(1, secs, greet_sec, 0)
-    pl.semaphore_wait(barrier, ctx - 1 + secs - 1)
+    pl.semaphore_wait(barrier, ctx - 1 + 3 * (secs - 1))
 
     def offset(k):
         half = groups // 2
@@ -124,56 +131,115 @@
             both = jnp.dot(weights, v2[...], preferred_element_type=F32)
             o_send[part(i), :] = (both[:, 0:HD] / both[:, HD:]).astype(BF)
         for j in (3, 2, 1, 0):
-            to = place(dz, j // 2, j % 2)
-            block = o_send.at[pl.ds(pl.multiple_of(to * rows, rows), rows)]
-
-            def remote(to=to, block=block):
-                pltpu.make_async_remote_copy(
-                    src_ref=block, dst_ref=att.at[:, my_cols], send_sem=send_o, recv_sem=recv_o,
-                    device_id={"ctx": to}, device_id_type=MESH,
-                ).start()
-
             if j:
-                remote()
+                give(0, dz, j)
             else:
-                pl.when(k < groups - 1)(remote)
+                pl.when(k < groups - 1)(functools.partial(give, 0, dz, j))
         return carry
 
+    def give(h, dz, j):
+        to = place(dz, j // 2, j % 2)
+        start, size = parts[h]
+        pltpu.make_async_remote_copy(
+            src_ref=o_send.at[pl.ds(pl.multiple_of(to * rows + start, 16), size)],
+            dst_ref=att.at[pl.ds(start, size), my_cols],
+            send_sem=send_o, recv_sem=recv_o.at[h],
+            device_id={"ctx": to}, device_id_type=MESH,
+        ).start()
+
+    def keep_own(h):
+        start, size = parts[h]
+        pltpu.make_async_copy(
+            o_send.at[pl.ds(pl.multiple_of(me * rows + start, 16), size)],
+            att.at[pl.ds(start, size), my_cols], recv_o.at[h]).start()
+
     lax.fori_loop(0, groups, attend, 0)
-    pltpu.make_async_copy(o_send.at[my_rows], att.at[:, my_cols], recv_o).start()
+    keep_own(0)
+    for h in range(1, len(parts)):
+        def rest(i, carry, h=h):
+            give(h, offset(i // 4), 3 - i % 4)
+            return carry
+
+        lax.fori_loop(0, ctx - 1, rest, 0)
+        keep_own(h)
 
     for load in loads:
         load.wait()
     now = step_ref[sec]
     shift, scale_up, gate = (mod[n, pl.ds(now, 1), :] for n in range(3))
-    pltpu.make_async_copy(att, att, recv_o).wait()
-    block = (hid[...].astype(F32) + gate * att[...].astype(F32)).astype(BF)
-    wide = block.astype(F32)
-    centre = jnp.mean(wide, axis=1, keepdims=True)
-    away = wide - centre
-    spread = jnp.mean(away * away, axis=1, keepdims=True)
-    normed = (away * lax.rsqrt(spread + 1e-06) * (1.0 + scale_up) + shift).astype(BF)
-    projected = jnp.dot(normed, down[...], preferred_element_type=F32).astype(BF)
-    cell = me * rows + lax.broadcasted_iota(jnp.int32, projected.shape, 0)
-    keep = cell < frames * CELLS
-    clip = jnp.where(keep, projected.astype(F32), 0.0)
-    proj[...] = clip.astype(BF)
-
-    below = lax.rem(me + ctx - 1, ctx)
-    above = lax.rem(me + 1, ctx)
-    up = pltpu.make_async_remote_copy(
-        src_ref=proj.at[pl.ds(rows - CELLS, CELLS)], dst_ref=lohalo, send_sem=send_h.at[0], recv_sem=recv_h.at[0],
+    source = jnp.int32(0)
+    for s in range(dest_ref.shape[0]):
+        source = jnp.where(dest_ref[s] == sec, s, source)
+
+    def adapt(h):
+        start, size = parts[h]
+        at = pl.ds(start, size)
+        pltpu.make_async_copy(att.at[at], att.at[at], recv_o.at[h]).wait()
+        block = (hid[at, :].astype(F32) + gate * att[at, :].astype(F32)).astype(BF)
+        wide = block.astype(F32)
+        centre = jnp.mean(wide, axis=1, keepdims=True)
+        away = wide - centre
+        spread = jnp.mean(away * away, axis=1, keepdims=True)
+        normed = (away * lax.rsqrt(spread + 1e-06) * (1.0 + scale_up) + shift).astype(BF)
+        projected = jnp.dot(normed, down[...], preferred_element_type=F32)
+        cell = me * rows + start + lax.broadcasted_iota(jnp.int32, projected.shape, 0)
+        proj[at, :] = jnp.where(cell < frames * CELLS, projected, 0.0).astype(BF)
+
+    boxes = (gathered_0, gathered_1)
+
+    def hand_off(h):
+        at = pl.ds(*parts[h])
+
+        def one(i, carry):
+            pltpu.make_async_remote_copy(
+                src_ref=proj.at[at], dst_ref=boxes[h].at[sec], send_sem=send_g.at[h], recv_sem=recv_g.at[h],
+                device_id={"sec": lax.rem(sec + i, secs)}, device_id_type=MESH,
+            ).start()
+            return carry
+
+        def beside(i, carry):
+            pltpu.make_async_remote_copy(
+                src_ref=proj.at[at], dst_ref=last_halo.at[sec], send_sem=send_h.at[2], recv_sem=recv_h.at[2],
+                device_id={"sec": lax.rem(sec + i, secs), "ctx": above}, device_id_type=MESH,
+            ).start()
+            return carry
+
+        if h == last:
+            lax.fori_loop(0, secs, beside, 0)
+        lax.fori_loop(1, secs, one, 0)
+        pltpu.make_async_copy(proj.at[at], boxes[h].at[sec], recv_g.at[h]).start()
+
+    def take(h):
+        pltpu.make_async_copy(boxes[h], boxes[h], recv_g.at[h]).wait()
+        clip_own[pl.ds(*parts[h]), :] = boxes[h][source]
+
+    before = CELLS - LATE
+    dn = pltpu.make_async_remote_copy(
+        src_ref=clip_own.at[pl.ds(0, CELLS)], dst_ref=hihalo, send_sem=send_h.at[0], recv_sem=recv_h.at[0],
+        device_id={"ctx": below}, device_id_type=MESH)
+    up = before and pltpu.make_async_remote_copy(
+        src_ref=clip_own.at[pl.ds(rows - CELLS, before)], dst_ref=lohalo, send_sem=send_h.at[1], recv_sem=recv_h.at[1],
         device_id={"ctx": above}, device_id_type=MESH)
-    dn = pltpu.make_async_remote_copy(
-        src_ref=proj.at[pl.ds(0, CELLS)], dst_ref=hihalo, send_sem=send_h.at[1], recv_sem=recv_h.at[1],
-        device_id={"ctx": below}, device_id_type=MESH)
-    up.start()
+
+    adapt(0)
+    hand_off(0)
+    adapt(1)
+    hand_off(1)
+    take(0)
     dn.start()
-    up.wait_recv()
+    if before:
+        up.start()
+    take(1)
     dn.wait_recv()
+    if before:
+        up.wait_recv()
+    pltpu.make_async_copy(last_halo, last_halo, recv_h.at[2]).wait()
 
     total_rows = rows + 2 * CELLS
-    xpad[0:CELLS, :] = jnp.where(me > 0, lohalo[...].astype(F32), 0.0)
+    clip = clip_own[...].astype(F32)
+    if before:
+        xpad[0:before, :] = jnp.where(me > 0, lohalo[...].astype(F32), 0.0)
+    xpad[before:CELLS, :] = jnp.where(me > 0, last_halo[source].astype(F32), 0.0)
     xpad[CELLS:CELLS + rows, :] = clip
     xpad[CELLS + rows:, :] = jnp.where(me < ctx - 1, hihalo[...].astype(F32), 0.0)
     padded = xpad[...]
@@ -188,32 +254,21 @@
             moved = jnp.where(inside, moved, 0.0).astype(BF)
             for a in range(3):
                 total += jnp.dot(moved[a * CELLS:a * CELLS + rows], conv[a * 9 + b * 3 + e], preferred_element_type=F32)
-    upbuf[...] = jnp.where(keep, total, 0.0).astype(BF)
-
-    def spread_out(i, carry):
-        pltpu.make_async_remote_copy(
-            src_ref=upbuf, dst_ref=gathered.at[sec], send_sem=send_g, recv_sem=recv_g,
-            device_id={"sec": lax.rem(sec + i, secs)}, device_id_type=MESH,
-        ).start()
-        return carry
-
-    lax.fori_loop(1, secs, spread_out, 0)
-    pltpu.make_async_copy(upbuf, gathered.at[sec], recv_g).start()
-
-    source = jnp.int32(0)
-    for s in range(dest_ref.shape[0]):
-        source = jnp.where(dest_ref[s] == sec, s, source)
+    cell = me * rows + lax.broadcasted_iota(jnp.int32, total.shape, 0)
+    out_ref[...] = jnp.where(cell < frames_ref[source] * CELLS, total, 0.0).astype(BF)
+
     others = pl.ds(0, (ctx - 1) * rows)
     pltpu.make_async_copy(kf.at[others], kf.at[others], send_k).wait()
     pltpu.make_async_copy(vf.at[others], vf.at[others], send_v).wait()
     pltpu.make_async_copy(qf.at[others], qf.at[others], send_q).wait()
     pltpu.make_async_copy(o_send.at[others], o_send.at[others], send_o).wait()
-    up.wait_send()
     dn.wait_send()
+    if before:
+        up.wait_send()
+    pltpu.make_async_copy(last_halo, last_halo, send_h.at[2]).wait()
     sent = pl.ds(0, secs - 1)
-    pltpu.make_async_copy(gathered.at[sent], gathered.at[sent], send_g).wait()
-    pltpu.make_async_copy(gathered, gathered, recv_g).wait()
-    out_ref[...] = gathered[source]
+    for h, box in enumerate(boxes):
+        pltpu.make_async_copy(box.at[sent], box.at[sent], send_g.at[h]).wait()
 
 
 def body(hidden, queries, keys, values, modulation, down_weight, conv_weight, clip_frames, destination, timestep):
@@ -222,6 +277,7 @@
     secs = lax.axis_size("sec")
     groups = lax.axis_size("ctx") // 4
     up = down_weight.shape[1]
+    late = min(LATE, CELLS)
     flat = lambda t: t.reshape(rows, width)
     smem = pl.BlockSpec(memory_space=pltpu.SMEM)
     anywhere = pl.BlockSpec(memory_space=pl.ANY)
@@ -239,11 +295,11 @@
             pltpu.VMEM((seq, HD), BF), pltpu.VMEM((rows, width), BF), pltpu.VMEM((rows, width), BF),
             pltpu.VMEM(modulation.shape, F32), pltpu.VMEM(down_weight.shape, BF), pltpu.VMEM(taps.shape, BF),
             pltpu.VMEM((rows, up), BF), pltpu.VMEM((rows + 2 * CELLS, up), F32),
-            pltpu.VMEM((CELLS, up), BF), pltpu.VMEM((CELLS, up), BF),
-            pltpu.VMEM((rows, up), BF), pltpu.VMEM((secs, rows, up), BF),
+            pltpu.VMEM((max(CELLS - late, 16), up), BF), pltpu.VMEM((CELLS, up), BF), pltpu.VMEM((secs, late, up), BF),
+            pltpu.VMEM((rows, up), BF), pltpu.VMEM((secs, rows - late, up), BF), pltpu.VMEM((secs, late, up), BF),
             pltpu.VMEM((2, SUB, seq), F32),
-            dma, dma, dma, dma, dma((2,)), dma,
-            dma, dma, dma((groups,)), dma, dma((2,)), dma, dma((4,)),
+            dma, dma, dma, dma, dma((3,)), dma((2,)),
+            dma, dma, dma((groups,)), dma((2,)), dma((3,)), dma((2,)), dma((4,)),
         ],
         compiler_params=pltpu.CompilerParams(
             collective_id=0, has_side_effects=True, vmem_limit_bytes=60 << 20

time: 121 us -> 117 us (0.967)
  Pallas kernels: 119 us -> 116 us
    pallas_call x1, Pallas kernels: 119 us -> 116 us  [body(): pl.pallas_call(kernel, out_shape=jax.ShapeDtypeStruct((rows, up), BF), in...]
where the time goes in v3:
time: 117 us
  Pallas kernels  116 us (99%)
  local copies, waits for them, and re-layouts  1.47 us (1%)
    pallas_call x1, Pallas kernels, body(): pl.pallas_call(kernel, out_shape=jax.ShapeDtypeStruct((rows, up), BF), in...  116 us

profile of v3, /device:TPU:1, one launch (start us, length us, event | category | flops | bytes accessed | tf_op | source)
XLA Modules:
  0.0 117.1 jit_solution(5162409792518934305)
XLA Ops:
  0.0 115.6 %section_kernel.1 = bf16[128,256]{1,0:T(8,128)(2,1)} custom-call(s32[8]{0:T(128)} %frames_ref.1, s32[8]{0:T(128)} %dest_ref.1, s32[8]{0:T(128)} %step_ref.1, bf16[128,4096]{1,0:T(8,128)(2,1)} %bitcast.9, bf16[128,4096]{1,0:T(8,128)(2,1)} %bitcast.10, bf16[128,4096]{1,0:T(8,128)(2,1)} %bitcast.11, bf16[128,4096]{1,0:T(8,128)(2,1)} %bitcast.12, ...), custom_call_target="tpu_custom_call" | custom-call | tf_op jit(solution)/shard_map/section_kernel/pallas_call | solution.py:287
  115.6 1.5 %copy.12 = bf16[1,128,256]{2,1,0:T(8,128)(2,1)} copy(bf16[1,128,256]{2,1,0:T(8,128)(2,1)} %bitcast.13) | data formatting | bytes 131072

commit v4 on v3

--- a/solution.py
+++ b/solution.py
@@ -59,8 +59,7 @@
     pl.semaphore_wait(barrier, ctx - 1 + 3 * (secs - 1))
 
     def offset(k):
-        half = groups // 2
-        return lax.rem(jnp.where(k % 2 == 0, half - k // 2, half + 1 + k // 2), groups)
+        return jnp.where(k == groups - 1, 0, jnp.where(k % 2 == 0, groups - 1 - k // 2, k // 2 + 1))
 
     my_rows = pl.ds(pl.multiple_of(me * rows, rows), rows)
     my_cols = pl.ds(pl.multiple_of(me * HD, HD), HD)
@@ -157,7 +156,7 @@
     keep_own(0)
     for h in range(1, len(parts)):
         def rest(i, carry, h=h):
-            give(h, offset(i // 4), 3 - i % 4)
+            give(h, offset(lax.rem(i, groups)), 3 - i // groups)
             return carry
 
         lax.fori_loop(0, ctx - 1, rest, 0)
@@ -193,7 +192,7 @@
         def one(i, carry):
             pltpu.make_async_remote_copy(
                 src_ref=proj.at[at], dst_ref=boxes[h].at[sec], send_sem=send_g.at[h], recv_sem=recv_g.at[h],
-                device_id={"sec": lax.rem(sec + i, secs)}, device_id_type=MESH,
+                device_id={"sec": lax.rem(sec + lax.rem(i * 3, secs), secs)}, device_id_type=MESH,
             ).start()
             return carry
 

time: 117 us -> 116 us (level)
  no operation moved by 1% of the time
where the time goes in v4:
time: 116 us
  Pallas kernels  115 us (99%)
  local copies, waits for them, and re-layouts  1.47 us (1%)
    pallas_call x1, Pallas kernels, body(): pl.pallas_call(kernel, out_shape=jax.ShapeDtypeStruct((rows, up), BF), in...  115 us

profile of v4, /device:TPU:1, one launch (start us, length us, event | category | flops | bytes accessed | tf_op | source)
XLA Modules:
  0.0 116.2 jit_solution(10128370780818249172)
XLA Ops:
  0.0 114.7 %section_kernel.1 = bf16[128,256]{1,0:T(8,128)(2,1)} custom-call(s32[8]{0:T(128)} %frames_ref.1, s32[8]{0:T(128)} %dest_ref.1, s32[8]{0:T(128)} %step_ref.1, bf16[128,4096]{1,0:T(8,128)(2,1)} %bitcast.9, bf16[128,4096]{1,0:T(8,128)(2,1)} %bitcast.10, bf16[128,4096]{1,0:T(8,128)(2,1)} %bitcast.11, bf16[128,4096]{1,0:T(8,128)(2,1)} %bitcast.12, ...), custom_call_target="tpu_custom_call" | custom-call | tf_op jit(solution)/shard_map/section_kernel/pallas_call | solution.py:286
  114.7 1.5 %copy.12 = bf16[1,128,256]{2,1,0:T(8,128)(2,1)} copy(bf16[1,128,256]{2,1,0:T(8,128)(2,1)} %bitcast.13) | data formatting | bytes 131072

commit v5 on v4

--- a/solution.py
+++ b/solution.py
@@ -49,14 +49,14 @@
         return carry
 
     def greet_sec(i, carry):
-        for place_at in (me, above, below):
+        for place_at in (me, below):
             pl.semaphore_signal(
                 barrier, inc=1, device_id={"sec": lax.rem(sec + i, secs), "ctx": place_at}, device_id_type=MESH)
         return carry
 
     lax.fori_loop(1, ctx, greet_ctx, 0)
     lax.fori_loop(1, secs, greet_sec, 0)
-    pl.semaphore_wait(barrier, ctx - 1 + 3 * (secs - 1))
+    pl.semaphore_wait(barrier, ctx - 1 + 2 * (secs - 1))
 
     def offset(k):
         return jnp.where(k == groups - 1, 0, jnp.where(k % 2 == 0, groups - 1 - k // 2, k // 2 + 1))

time: 116 us -> 117 us (level); the launches traced: 116 us -> 116 us
  no operation moved by 1% of the time
where the time goes in v5:
time: 117 us; the launch traced here: 116 us
  Pallas kernels  114 us (97%)
  local copies, waits for them, and re-layouts  1.47 us (1%)
    pallas_call x1, Pallas kernels, body(): pl.pallas_call(kernel, out_shape=jax.ShapeDtypeStruct((rows, up), BF), in...  114 us

profile of v5, /device:TPU:1, one launch (start us, length us, event | category | flops | bytes accessed | tf_op | source)
XLA Modules:
  0.0 115.8 jit_solution(6574845150688013489)
XLA Ops:
  0.0 114.3 %section_kernel.1 = bf16[128,256]{1,0:T(8,128)(2,1)} custom-call(s32[8]{0:T(128)} %frames_ref.1, s32[8]{0:T(128)} %dest_ref.1, s32[8]{0:T(128)} %step_ref.1, bf16[128,4096]{1,0:T(8,128)(2,1)} %bitcast.9, bf16[128,4096]{1,0:T(8,128)(2,1)} %bitcast.10, bf16[128,4096]{1,0:T(8,128)(2,1)} %bitcast.11, bf16[128,4096]{1,0:T(8,128)(2,1)} %bitcast.12, ...), custom_call_target="tpu_custom_call" | custom-call | tf_op jit(solution)/shard_map/section_kernel/pallas_call | solution.py:286
  114.3 1.5 %copy.12 = bf16[1,128,256]{2,1,0:T(8,128)(2,1)} copy(bf16[1,128,256]{2,1,0:T(8,128)(2,1)} %bitcast.13) | data formatting | bytes 131072
